TPU v7x, 256 devices: a whole 4x4x8 slice. The times are simulated.
256 devices in a mesh: tm: 16 (over y, x), space: 16 (over z, core).
Axes of the slice: x: 4, y: 4, z: 8, core: 2. Of those that a mesh axis runs over, the one named last changes fastest.
Arguments:
- base_start: float32 [16, 512, 4096], P('tm', 'space'), may hold values from -6 to 6
- direction: float32 [16, 512, 4096], P('tm', 'space'), may hold values from -6 to 6
- damp_levels: int32 [64, 32], P('space'), may hold values from 0 to 3
- damp_table: float32 [4], replicated, may hold values from 0.1 to 2
Outputs:
- product: float32 [16, 512, 4096], P('tm', 'space')
All inputs are finite; a program needn't handle non-finite values.
Results may differ from a plain program's by a relative error of at most 0.00002.
Values sent between devices are 32-bit elements; how exact they have to be, the bound alone decides.
A program may use at most 64 MiB of HBM per device.

v0:
```python
import jax
import jax.numpy as jnp
from jax import lax
from jax.sharding import PartitionSpec as P

STEPS = 4


coef_lap = 0.05
coef_bih = 0.028
coef_slope = 0.05


def with_halo(shard, sides, width):
    for axis, dim in sides:
        count, length = (lax.axis_size(axis), shard.shape[dim])
        up = [(i, (i + 1) % count) for i in range(count)]
        down = [(j, i) for i, j in up]
        last = lax.slice_in_dim(shard, length - width, length, axis=dim)
        leading = lax.slice_in_dim(shard, 0, width, axis=dim)
        before = lax.ppermute(last, axis, up)
        after = lax.ppermute(leading, axis, down)
        shard = jnp.concatenate([before, shard, after], axis=dim)
    return shard


def shifted(block, axis, distance):
    devices = range(lax.axis_size(axis))
    route = [((i - distance) % len(devices), i) for i in devices]
    return lax.ppermute(block, axis, route)


def shave(field, depth):
    return field[..., depth : field.shape[-2] - depth, :]


def laplace(padded):
    center = padded[..., 1:-1, :]
    return (
        padded[..., 2:, :]
        + padded[..., :-2, :]
        + jnp.roll(center, 1, -1)
        + jnp.roll(center, -1, -1)
        - 4.0 * center
    )


def slope_cols(padded):
    center = padded[..., 1:-1, :]
    return (jnp.roll(center, -1, -1) - jnp.roll(center, 1, -1)) * 0.5


def slope_rows(padded):
    return (padded[..., 2:, :] - padded[..., :-2, :]) * 0.5


def base_step(padded):
    first = laplace(padded)
    second = laplace(first)
    along_x = shave(slope_cols(padded), 1)
    along_y = shave(slope_rows(padded), 1)
    return (
        shave(padded, 2)
        - coef_lap * shave(first, 1)
        - coef_bih * second
        - coef_slope * (along_x * along_x + along_y * along_y)
    )


def tangent_step(base_pad, pert_pad):
    first = laplace(pert_pad)
    second = laplace(first)
    cross = shave(slope_cols(base_pad), 1) * shave(slope_cols(pert_pad), 1) + shave(
        slope_rows(base_pad), 1
    ) * shave(slope_rows(pert_pad), 1)
    return (
        shave(pert_pad, 2)
        - coef_lap * shave(first, 1)
        - coef_bih * second
        - 2.0 * coef_slope * cross
    )


def adjoint_step(base_pad, dual_pad):
    first = laplace(dual_pad)
    second = laplace(first)
    inner = shave(dual_pad, 1)
    flux_x = slope_cols(base_pad) * inner
    flux_y = slope_rows(base_pad) * inner
    spread = slope_cols(flux_x) + slope_rows(flux_y)
    return (
        shave(dual_pad, 2)
        - coef_lap * shave(first, 1)
        - coef_bih * second
        + 2.0 * coef_slope * spread
    )


def adjoint_chain(dual, stored, count):
    for step in range(count - 1, -1, -1):
        dual_pad = with_halo(dual, (("space", 0),), 2)
        dual = adjoint_step(stored[step], dual_pad)
    return dual


def shards(base_start, direction, damp_levels, damp_table):
    start_pert = direction[0]
    following = shifted(direction, "tm", -1)[0]
    stored = []
    dual = None
    state = base_start[0]
    pert = start_pert
    for step in range(STEPS):
        padded = with_halo(jnp.stack([state, pert]), (("space", 1),), 2)
        stored.append(padded[0])
        pert = tangent_step(padded[0], padded[1])
        state = base_step(padded[0])
    resid = pert - following
    resid_prev = shifted(resid[None], "tm", 1)[0]
    dual = adjoint_chain(resid, stored, STEPS)
    levels = jnp.arange(damp_table.shape[0])
    coarse = jnp.sum(
        jnp.where(damp_levels[..., None] == levels, damp_table, jnp.zeros_like(damp_table)), -1
    )
    damp = jnp.repeat(jnp.repeat(coarse, 8, 0), 128, 1)
    result = dual - resid_prev + damp * start_pert
    return result[None]


def solution(mesh):
    in_specs = (P("tm", "space", None), P("tm", "space", None), P("space", None), P())
    out_specs = P("tm", "space", None)
    return jax.shard_map(shards, mesh=mesh, in_specs=in_specs, out_specs=out_specs, check_vma=False)
```

profile of v0, /device:TPU:97, one launch (start us, length us, event | category | flops | bytes accessed | tf_op | source)
XLA Modules:
  0.0 91.5 jit_solution(6136693021328016364)
XLA Ops:
  0.0 1.1 %constant_dynamic-update-slice_fusion.1 = f32[2,32,4096]{2,1,0:T(8,128)S(1)} fusion(f32[1,32,4096]{2,1,0:T(8,128)} %param.4), kind=kLoop, calls=%fused_computation.300 | loop fusion | bytes 1048576
  1.3 3.4 %collective-permute-start.1 = (f32[2,2,4096]{2,1,0:T(2,128)S(1)}, f32[2,2,4096]{2,1,0:T(2,128)S(1)}, u32[]{:S(2)}, u32[]{:S(2)}) collective-permute-start(f32[2,2,4096]{2,1,0:T(2,128)S(1)} %get-tuple-element.44), channel_id=1, source_target_pairs={{0,1},{1,2},{2,3},{3,4},{4,5},{5,6},{6,7},{7,8},{8,9},{9,10},{10,1... | collective-permute-start | bytes 196616 | tf_op jit(solution)/shard_map/ppermute | solution.py:21
  4.7 1.3 %collective-permute-done.1 = f32[2,2,4096]{2,1,0:T(2,128)S(1)} collective-permute-done((f32[2,2,4096]{2,1,0:T(2,128)S(1)}, f32[2,2,4096]{2,1,0:T(2,128)S(1)}, u32[]{:S(2)}, u32[]{:S(2)}) %collective-permute-start.1) | collective-permute-done | bytes 65568 | tf_op jit(solution)/shard_map/ppermute | solution.py:21
  6.0 3.6 %collective-permute-done = f32[2,2,4096]{2,1,0:T(2,128)S(1)} collective-permute-done((f32[2,2,4096]{2,1,0:T(2,128)S(1)}, f32[2,2,4096]{2,1,0:T(2,128)S(1)}, u32[]{:S(2)}, u32[]{:S(2)}) %collective-permute-start) | collective-permute-done | bytes 65568 | tf_op jit(solution)/shard_map/ppermute | solution.py:22
  11.9 0.9 %copy-done.1 = f32[1,32,4096]{2,1,0:T(8,128)S(1)} copy-done((f32[1,32,4096]{2,1,0:T(8,128)S(1)}, f32[1,32,4096]{2,1,0:T(8,128)}, u32[]{:S(2)}) %copy-start.1) | copy-done | bytes 524312
  13.2 0.7 fusion.73
  14.1 2.9 %collective-permute-start.3 = (f32[2,2,4096]{2,1,0:T(2,128)S(1)}, f32[2,2,4096]{2,1,0:T(2,128)S(1)}, u32[]{:S(2)}, u32[]{:S(2)}) collective-permute-start(f32[2,2,4096]{2,1,0:T(2,128)S(1)} %get-tuple-element.43), channel_id=1, source_target_pairs={{0,1},{1,2},{2,3},{3,4},{4,5},{5,6},{6,7},{7,8},{8,9},{9,10},{10,1... | collective-permute-start | bytes 196616 | tf_op jit(solution)/shard_map/ppermute | solution.py:21
  17.0 1.9 %collective-permute-done.2 = f32[2,2,4096]{2,1,0:T(2,128)S(1)} collective-permute-done((f32[2,2,4096]{2,1,0:T(2,128)S(1)}, f32[2,2,4096]{2,1,0:T(2,128)S(1)}, u32[]{:S(2)}, u32[]{:S(2)}) %collective-permute-start.2) | collective-permute-done | bytes 65568 | tf_op jit(solution)/shard_map/ppermute | solution.py:22
  21.9 0.7 fusion.65
  22.7 3.0 %collective-permute-start.5 = (f32[2,2,4096]{2,1,0:T(2,128)S(1)}, f32[2,2,4096]{2,1,0:T(2,128)S(1)}, u32[]{:S(2)}, u32[]{:S(2)}) collective-permute-start(f32[2,2,4096]{2,1,0:T(2,128)S(1)} %get-tuple-element.39), channel_id=1, source_target_pairs={{0,1},{1,2},{2,3},{3,4},{4,5},{5,6},{6,7},{7,8},{8,9},{9,10},{10,1... | collective-permute-start | bytes 196616 | tf_op jit(solution)/shard_map/ppermute | solution.py:21
  25.6 1.9 %collective-permute-done.4 = f32[2,2,4096]{2,1,0:T(2,128)S(1)} collective-permute-done((f32[2,2,4096]{2,1,0:T(2,128)S(1)}, f32[2,2,4096]{2,1,0:T(2,128)S(1)}, u32[]{:S(2)}, u32[]{:S(2)}) %collective-permute-start.4) | collective-permute-done | bytes 65568 | tf_op jit(solution)/shard_map/ppermute | solution.py:22
  30.4 0.7 fusion.57
  31.3 3.0 %collective-permute-start.7 = (f32[2,2,4096]{2,1,0:T(2,128)S(1)}, f32[2,2,4096]{2,1,0:T(2,128)S(1)}, u32[]{:S(2)}, u32[]{:S(2)}) collective-permute-start(f32[2,2,4096]{2,1,0:T(2,128)S(1)} %get-tuple-element.35), channel_id=1, source_target_pairs={{0,1},{1,2},{2,3},{3,4},{4,5},{5,6},{6,7},{7,8},{8,9},{9,10},{10,1... | collective-permute-start | bytes 196616 | tf_op jit(solution)/shard_map/ppermute | solution.py:21
  34.2 4.9 %collective-permute-start.8 = (f32[1,32,4096]{2,1,0:T(8,128)S(1)}, f32[1,32,4096]{2,1,0:T(8,128)S(1)}, u32[]{:S(2)}, u32[]{:S(2)}) collective-permute-start(f32[1,32,4096]{2,1,0:T(8,128)S(1)} %copy-done), channel_id=1, source_target_pairs={{16,0},{32,16},{48,32},{64,48},{80,64},{96,80},{112,96},{128,112},... | collective-permute-start | bytes 1572872 | tf_op jit(solution)/shard_map/ppermute | solution.py:30
  41.3 7.6 %collective-permute-done.8 = f32[1,32,4096]{2,1,0:T(8,128)S(1)} collective-permute-done((f32[1,32,4096]{2,1,0:T(8,128)S(1)}, f32[1,32,4096]{2,1,0:T(8,128)S(1)}, u32[]{:S(2)}, u32[]{:S(2)}) %collective-permute-start.8) | collective-permute-done | bytes 524320 | tf_op jit(solution)/shard_map/ppermute | solution.py:30
  48.9 0.7 fusion.49
  49.7 2.4 %collective-permute-start.10 = (f32[2,4096]{1,0:T(2,128)S(1)}, f32[2,4096]{1,0:T(2,128)S(1)}, u32[]{:S(2)}, u32[]{:S(2)}) collective-permute-start(f32[2,4096]{1,0:T(2,128)S(1)} %get-tuple-element.164), channel_id=1, source_target_pairs={{0,1},{1,2},{2,3},{3,4},{4,5},{5,6},{6,7},{7,8},{8,9},{9,10},{10,1... | collective-permute-start | bytes 98312 | tf_op jit(solution)/shard_map/ppermute | solution.py:21
  52.1 1.0 %collective-permute-done.10 = f32[2,4096]{1,0:T(2,128)S(1)} collective-permute-done((f32[2,4096]{1,0:T(2,128)S(1)}, f32[2,4096]{1,0:T(2,128)S(1)}, u32[]{:S(2)}, u32[]{:S(2)}) %collective-permute-start.10) | collective-permute-done | bytes 32800 | tf_op jit(solution)/shard_map/ppermute | solution.py:21
  53.1 3.5 %collective-permute-done.9 = f32[2,4096]{1,0:T(2,128)S(1)} collective-permute-done((f32[2,4096]{1,0:T(2,128)S(1)}, f32[2,4096]{1,0:T(2,128)S(1)}, u32[]{:S(2)}, u32[]{:S(2)}) %collective-permute-start.9) | collective-permute-done | bytes 32800 | tf_op jit(solution)/shard_map/ppermute | solution.py:22
  59.7 3.4 %collective-permute-done.11 = f32[2,4096]{1,0:T(2,128)S(1)} collective-permute-done((f32[2,4096]{1,0:T(2,128)S(1)}, f32[2,4096]{1,0:T(2,128)S(1)}, u32[]{:S(2)}, u32[]{:S(2)}) %collective-permute-start.11) | collective-permute-done | bytes 32800 | tf_op jit(solution)/shard_map/ppermute | solution.py:22
  66.2 3.4 %collective-permute-done.13 = f32[2,4096]{1,0:T(2,128)S(1)} collective-permute-done((f32[2,4096]{1,0:T(2,128)S(1)}, f32[2,4096]{1,0:T(2,128)S(1)}, u32[]{:S(2)}, u32[]{:S(2)}) %collective-permute-start.13) | collective-permute-done | bytes 32800 | tf_op jit(solution)/shard_map/ppermute | solution.py:22
  72.6 3.4 %collective-permute-done.15 = f32[2,4096]{1,0:T(2,128)S(1)} collective-permute-done((f32[2,4096]{1,0:T(2,128)S(1)}, f32[2,4096]{1,0:T(2,128)S(1)}, u32[]{:S(2)}, u32[]{:S(2)}) %collective-permute-start.15) | collective-permute-done | bytes 32800 | tf_op jit(solution)/shard_map/ppermute | solution.py:22
  77.2 12.5 %collective-permute-done.17 = f32[1,32,4096]{2,1,0:T(8,128)S(1)} collective-permute-done((f32[1,32,4096]{2,1,0:T(8,128)S(1)}, f32[1,32,4096]{2,1,0:T(8,128)S(1)}, u32[]{:S(2)}, u32[]{:S(2)}) %collective-permute-start.17) | collective-permute-done | bytes 524320 | tf_op jit(solution)/shard_map/ppermute | solution.py:30
  89.9 1.6 %fusion.76 = f32[1,32,4096]{2,1,0:T(8,128)} fusion(f32[4,8,32,128]{3,2,1,0:T(8,128)S(1)} %bitcast.146, f32[34,4096]{1,0:T(8,128)S(1)} %get-tuple-element.51, f32[34,4096]{1,0:T(8,128)S(1)} %get-tuple-element.52, f32[32,4095]{1,0:T(8,128)S(1)} %get-tuple-element.54, f32[32,1]{1,0:T(8,128)S(1)} %get-tuple-element.56, f32[32,1]{1,0:T(8,128)S(1)} %get-tuple-element.55, ...), kind=kLoop, calls=%fused_computation.174 | loop fusion | flops 2752512 | bytes 7340032 | tf_op jit(solution)/shard_map/broadcast_in_dim | solution.py:127
  (121 shorter events, 21.4 us)
Async XLA Ops:
  0.0 1.2 %copy-start = (f32[1,32,4096]{2,1,0:T(8,128)S(1)}, f32[1,32,4096]{2,1,0:T(8,128)}, u32[]{:S(2)}) copy-start(f32[1,32,4096]{2,1,0:T(8,128)} %param.5) | copy-start | bytes 1572868
  1.3 4.8 %collective-permute-start.1 = (f32[2,2,4096]{2,1,0:T(2,128)S(1)}, f32[2,2,4096]{2,1,0:T(2,128)S(1)}, u32[]{:S(2)}, u32[]{:S(2)}) collective-permute-start(f32[2,2,4096]{2,1,0:T(2,128)S(1)} %get-tuple-element.44), channel_id=1, source_target_pairs={{0,1},{1,2},{2,3},{3,4},{4,5},{5,6},{6,7},{7,8},{8,9},{9,10},{10,1... | collective-permute-start | bytes 196616 | tf_op jit(solution)/shard_map/ppermute | solution.py:21
  4.7 4.9 %collective-permute-start = (f32[2,2,4096]{2,1,0:T(2,128)S(1)}, f32[2,2,4096]{2,1,0:T(2,128)S(1)}, u32[]{:S(2)}, u32[]{:S(2)}) collective-permute-start(f32[2,2,4096]{2,1,0:T(2,128)S(1)} %get-tuple-element.45), channel_id=1, source_target_pairs={{1,0},{2,1},{3,2},{4,3},{5,4},{6,5},{7,6},{8,7},{9,8},{10,9},{11,1... | collective-permute-start | bytes 196616 | tf_op jit(solution)/shard_map/ppermute | solution.py:22
  11.8 1.0 %copy-start.1 = (f32[1,32,4096]{2,1,0:T(8,128)S(1)}, f32[1,32,4096]{2,1,0:T(8,128)}, u32[]{:S(2)}) copy-start(f32[1,32,4096]{2,1,0:T(8,128)} %param.4) | copy-start | bytes 1572868
  14.0 4.9 %collective-permute-start.2 = (f32[2,2,4096]{2,1,0:T(2,128)S(1)}, f32[2,2,4096]{2,1,0:T(2,128)S(1)}, u32[]{:S(2)}, u32[]{:S(2)}) collective-permute-start(f32[2,2,4096]{2,1,0:T(2,128)S(1)} %get-tuple-element.42), channel_id=1, source_target_pairs={{1,0},{2,1},{3,2},{4,3},{5,4},{6,5},{7,6},{8,7},{9,8},{10,9},{11,1... | collective-permute-start | bytes 196616 | tf_op jit(solution)/shard_map/ppermute | solution.py:22
  14.1 4.9 %collective-permute-start.3 = (f32[2,2,4096]{2,1,0:T(2,128)S(1)}, f32[2,2,4096]{2,1,0:T(2,128)S(1)}, u32[]{:S(2)}, u32[]{:S(2)}) collective-permute-start(f32[2,2,4096]{2,1,0:T(2,128)S(1)} %get-tuple-element.43), channel_id=1, source_target_pairs={{0,1},{1,2},{2,3},{3,4},{4,5},{5,6},{6,7},{7,8},{8,9},{9,10},{10,1... | collective-permute-start | bytes 196616 | tf_op jit(solution)/shard_map/ppermute | solution.py:21
  22.7 4.9 %collective-permute-start.4 = (f32[2,2,4096]{2,1,0:T(2,128)S(1)}, f32[2,2,4096]{2,1,0:T(2,128)S(1)}, u32[]{:S(2)}, u32[]{:S(2)}) collective-permute-start(f32[2,2,4096]{2,1,0:T(2,128)S(1)} %get-tuple-element.38), channel_id=1, source_target_pairs={{1,0},{2,1},{3,2},{4,3},{5,4},{6,5},{7,6},{8,7},{9,8},{10,9},{11,1... | collective-permute-start | bytes 196616 | tf_op jit(solution)/shard_map/ppermute | solution.py:22
  22.7 4.9 %collective-permute-start.5 = (f32[2,2,4096]{2,1,0:T(2,128)S(1)}, f32[2,2,4096]{2,1,0:T(2,128)S(1)}, u32[]{:S(2)}, u32[]{:S(2)}) collective-permute-start(f32[2,2,4096]{2,1,0:T(2,128)S(1)} %get-tuple-element.39), channel_id=1, source_target_pairs={{0,1},{1,2},{2,3},{3,4},{4,5},{5,6},{6,7},{7,8},{8,9},{9,10},{10,1... | collective-permute-start | bytes 196616 | tf_op jit(solution)/shard_map/ppermute | solution.py:21
  31.2 7.9 %collective-permute-start.6 = (f32[2,2,4096]{2,1,0:T(2,128)S(1)}, f32[2,2,4096]{2,1,0:T(2,128)S(1)}, u32[]{:S(2)}, u32[]{:S(2)}) collective-permute-start(f32[2,2,4096]{2,1,0:T(2,128)S(1)} %get-tuple-element.34), channel_id=1, source_target_pairs={{1,0},{2,1},{3,2},{4,3},{5,4},{6,5},{7,6},{8,7},{9,8},{10,9},{11,1... | collective-permute-start | bytes 196616 | tf_op jit(solution)/shard_map/ppermute | solution.py:22
  31.3 7.9 %collective-permute-start.7 = (f32[2,2,4096]{2,1,0:T(2,128)S(1)}, f32[2,2,4096]{2,1,0:T(2,128)S(1)}, u32[]{:S(2)}, u32[]{:S(2)}) collective-permute-start(f32[2,2,4096]{2,1,0:T(2,128)S(1)} %get-tuple-element.35), channel_id=1, source_target_pairs={{0,1},{1,2},{2,3},{3,4},{4,5},{5,6},{6,7},{7,8},{8,9},{9,10},{10,1... | collective-permute-start | bytes 196616 | tf_op jit(solution)/shard_map/ppermute | solution.py:21
  34.2 14.7 %collective-permute-start.8 = (f32[1,32,4096]{2,1,0:T(8,128)S(1)}, f32[1,32,4096]{2,1,0:T(8,128)S(1)}, u32[]{:S(2)}, u32[]{:S(2)}) collective-permute-start(f32[1,32,4096]{2,1,0:T(8,128)S(1)} %copy-done), channel_id=1, source_target_pairs={{16,0},{32,16},{48,32},{64,48},{80,64},{96,80},{112,96},{128,112},... | collective-permute-start | bytes 1572872 | tf_op jit(solution)/shard_map/ppermute | solution.py:30
  49.7 3.4 %collective-permute-start.10 = (f32[2,4096]{1,0:T(2,128)S(1)}, f32[2,4096]{1,0:T(2,128)S(1)}, u32[]{:S(2)}, u32[]{:S(2)}) collective-permute-start(f32[2,4096]{1,0:T(2,128)S(1)} %get-tuple-element.164), channel_id=1, source_target_pairs={{0,1},{1,2},{2,3},{3,4},{4,5},{5,6},{6,7},{7,8},{8,9},{9,10},{10,1... | collective-permute-start | bytes 98312 | tf_op jit(solution)/shard_map/ppermute | solution.py:21
  52.1 4.6 %collective-permute-start.9 = (f32[2,4096]{1,0:T(2,128)S(1)}, f32[2,4096]{1,0:T(2,128)S(1)}, u32[]{:S(2)}, u32[]{:S(2)}) collective-permute-start(f32[2,4096]{1,0:T(2,128)S(1)} %get-tuple-element.165), channel_id=1, source_target_pairs={{1,0},{2,1},{3,2},{4,3},{5,4},{6,5},{7,6},{8,7},{9,8},{10,9},{11,1... | collective-permute-start | bytes 98312 | tf_op jit(solution)/shard_map/ppermute | solution.py:22
  58.5 1.2 %collective-permute-start.12 = (f32[2,4096]{1,0:T(2,128)S(1)}, f32[2,4096]{1,0:T(2,128)S(1)}, u32[]{:S(2)}, u32[]{:S(2)}) collective-permute-start(f32[2,4096]{1,0:T(2,128)S(1)} %get-tuple-element.162), channel_id=1, source_target_pairs={{0,1},{1,2},{2,3},{3,4},{4,5},{5,6},{6,7},{7,8},{8,9},{9,10},{10,1... | collective-permute-start | bytes 98312 | tf_op jit(solution)/shard_map/ppermute | solution.py:21
  58.5 4.6 %collective-permute-start.11 = (f32[2,4096]{1,0:T(2,128)S(1)}, f32[2,4096]{1,0:T(2,128)S(1)}, u32[]{:S(2)}, u32[]{:S(2)}) collective-permute-start(f32[2,4096]{1,0:T(2,128)S(1)} %get-tuple-element.163), channel_id=1, source_target_pairs={{1,0},{2,1},{3,2},{4,3},{5,4},{6,5},{7,6},{8,7},{9,8},{10,9},{11,1... | collective-permute-start | bytes 98312 | tf_op jit(solution)/shard_map/ppermute | solution.py:22
  64.4 1.1 %copy-start.2 = (s32[4,32]{1,0:T(4,128)S(1)}, s32[4,32]{1,0:T(4,128)}, u32[]{:S(2)}) copy-start(s32[4,32]{1,0:T(4,128)} %param.6) | copy-start | bytes 1540
  64.4 1.1 %copy-start.3 = (f32[4]{0:T(128)S(1)}, f32[4]{0:T(128)}, u32[]{:S(2)}) copy-start(f32[4]{0:T(128)} %param.7) | copy-start | bytes 52
  64.9 1.2 %collective-permute-start.14 = (f32[2,4096]{1,0:T(2,128)S(1)}, f32[2,4096]{1,0:T(2,128)S(1)}, u32[]{:S(2)}, u32[]{:S(2)}) collective-permute-start(f32[2,4096]{1,0:T(2,128)S(1)} %get-tuple-element.160), channel_id=1, source_target_pairs={{0,1},{1,2},{2,3},{3,4},{4,5},{5,6},{6,7},{7,8},{8,9},{9,10},{10,1... | collective-permute-start | bytes 98312 | tf_op jit(solution)/shard_map/ppermute | solution.py:21
  65.0 4.6 %collective-permute-start.13 = (f32[2,4096]{1,0:T(2,128)S(1)}, f32[2,4096]{1,0:T(2,128)S(1)}, u32[]{:S(2)}, u32[]{:S(2)}) collective-permute-start(f32[2,4096]{1,0:T(2,128)S(1)} %get-tuple-element.161), channel_id=1, source_target_pairs={{1,0},{2,1},{3,2},{4,3},{5,4},{6,5},{7,6},{8,7},{9,8},{10,9},{11,1... | collective-permute-start | bytes 98312 | tf_op jit(solution)/shard_map/ppermute | solution.py:22
  71.4 1.2 %collective-permute-start.16 = (f32[2,4096]{1,0:T(2,128)S(1)}, f32[2,4096]{1,0:T(2,128)S(1)}, u32[]{:S(2)}, u32[]{:S(2)}) collective-permute-start(f32[2,4096]{1,0:T(2,128)S(1)} %get-tuple-element.158), channel_id=1, source_target_pairs={{0,1},{1,2},{2,3},{3,4},{4,5},{5,6},{6,7},{7,8},{8,9},{9,10},{10,1... | collective-permute-start | bytes 98312 | tf_op jit(solution)/shard_map/ppermute | solution.py:21
  71.4 4.6 %collective-permute-start.15 = (f32[2,4096]{1,0:T(2,128)S(1)}, f32[2,4096]{1,0:T(2,128)S(1)}, u32[]{:S(2)}, u32[]{:S(2)}) collective-permute-start(f32[2,4096]{1,0:T(2,128)S(1)} %get-tuple-element.159), channel_id=1, source_target_pairs={{1,0},{2,1},{3,2},{4,3},{5,4},{6,5},{7,6},{8,7},{9,8},{10,9},{11,1... | collective-permute-start | bytes 98312 | tf_op jit(solution)/shard_map/ppermute | solution.py:22
  71.9 17.8 %collective-permute-start.17 = (f32[1,32,4096]{2,1,0:T(8,128)S(1)}, f32[1,32,4096]{2,1,0:T(8,128)S(1)}, u32[]{:S(2)}, u32[]{:S(2)}) collective-permute-start(f32[1,32,4096]{2,1,0:T(8,128)S(1)} %bitcast.145), channel_id=1, source_target_pairs={{240,0},{0,16},{16,32},{32,48},{48,64},{64,80},{80,96},{96,112},{1... | collective-permute-start | bytes 1572872 | tf_op jit(solution)/shard_map/ppermute | solution.py:30
where the time goes:
time: 91.7 us; the launch traced here: 91.5 us
  waiting for transfers between devices  45.5 us (50%)
  starting transfers between devices  21.2 us (23%)
  other arithmetic  13.8 us (15%)
  local copies, waits for them, and re-layouts  10.6 us (12%)
    ppermute x8, waiting for transfers between devices, with_halo(): after = lax.ppermute(leading, axis, down)  21.1 us
    ppermute x2, waiting for transfers between devices, shifted(): return lax.ppermute(block, axis, route)  20 us
    ppermute x8, starting transfers between devices, with_halo(): before = lax.ppermute(last, axis, up)  14.8 us
    slice x32, local copies, waits for them, and re-layouts, laplace(): jnp.roll(center, -1, -1)  5.22 us
    ppermute x2, starting transfers between devices, shifted(): return lax.ppermute(block, axis, route)  4.93 us
    ppermute x8, waiting for transfers between devices, with_halo(): before = lax.ppermute(last, axis, up)  4.35 us
    sub x3, other arithmetic, tangent_step(): shave(pert_pad, 2) - coef_lap * shave(first, 1) - coef_bih * second  2.18 us
    unnamed x9, local copies, waits for them, and re-layouts  2.13 us
  transfers between devices with their start and end apart: 18, of which 14 were waited for; matrix products, arithmetic and copies ran while one was open for 4% of the time, Pallas kernels for 0%

commit v1 on v0

v1 whole, which is shorter than its diff:
```python
import functools
import math

import jax
import jax.numpy as jnp
from jax import lax
from jax.experimental import pallas as pl
from jax.experimental.pallas import tpu as pltpu
from jax.sharding import PartitionSpec as P

MESH = pl.DeviceIdType.MESH

STEPS = 4
ROWS = 32
COLS = 4096
LANES = 128
CHUNKS = COLS // LANES
OFF = 16
HELD = ROWS + 2 * OFF

coef_lap = 0.05
coef_bih = 0.028
coef_slope = 0.05

_root = math.sqrt((coef_lap / coef_bih) ** 2 + 4.0 / coef_bih)
NEAR = 4.0 + (-coef_lap / coef_bih + _root) / 2.0
FAR = 4.0 + (-coef_lap / coef_bih - _root) / 2.0
SLOPE = coef_slope / (2.0 * coef_bih)
SCALE = coef_bih**STEPS


def beside(x):
    lane = lax.broadcasted_iota(jnp.int32, (1, 1, LANES), 2)
    right = pltpu.roll(x, LANES - 1, 2)
    left = pltpu.roll(x, 1, 2)
    right_next = jnp.concatenate([right[:, 8:], pltpu.roll(right[:, :8], 7, 1)], 1)
    left_next = jnp.concatenate([pltpu.roll(left[:, 24:], 1, 1), left[:, :24]], 1)
    return (
        jnp.where(lane == LANES - 1, right_next, right),
        jnp.where(lane == 0, left_next, left),
    )


def over_rows(low, high, most, body):
    count = high - low + 1
    steps = -(-count // most)
    size = -(-count // steps)

    def step(i, carry):
        for j in range(size):
            body(low + OFF + i * size + j)
        return carry

    if steps == 1:
        step(0, 0)
    else:
        lax.fori_loop(0, steps, step, 0)


def cross_of(ref, r):
    return ref[pl.ds(r, 1)], ref[pl.ds(r - 1, 1)], ref[pl.ds(r + 1, 1)]


def forward_first(k, b, low, high, most, base=True, tangent=True):
    state, half, grad_x, grad_y = b.state.at[k], b.state_half.at[k], b.grad_x.at[k], b.grad_y.at[k]
    pert, pert_half, cross = b.pert.at[k], b.pert_half.at[k], b.cross.at[k]

    def body(r):
        row = pl.ds(r, 1)
        c, n, s = cross_of(state, r)
        right, left = beside(c)
        slope_x, slope_y = right - left, s - n
        grad_x[row] = slope_x
        grad_y[row] = slope_y
        if base:
            half[row] = ((right + left) + (n + s)) - NEAR * c
        if tangent:
            c, n, s = cross_of(pert, r)
            right, left = beside(c)
            pert_half[row] = ((right + left) + (n + s)) - NEAR * c
            cross[row] = slope_x * (right - left) + slope_y * (s - n)

    over_rows(low, high, most, body)


def forward_second(k, b, low, high, most, base=True, tangent=True):
    half, grad_x, grad_y = b.state_half.at[k], b.grad_x.at[k], b.grad_y.at[k]
    pert_half, cross, pert_next = b.pert_half.at[k], b.cross.at[k], b.pert.at[k + 1]
    if base:
        state_next = b.state.at[k + 1]

    def body(r):
        row = pl.ds(r, 1)
        if base:
            c, n, s = cross_of(half, r)
            right, left = beside(c)
            slope_x, slope_y = grad_x[row], grad_y[row]
            linear = ((right + left) + (n + s)) - FAR * c
            squares = slope_x * slope_x + slope_y * slope_y
            state_next[row] = linear * (-coef_bih) + squares * (-coef_bih / 2.0)
        if tangent:
            c, n, s = cross_of(pert_half, r)
            right, left = beside(c)
            pert_next[row] = (((right + left) + (n + s)) - FAR * c) + cross[row]

    over_rows(low, high, most, body)


def adjoint_first(k, b, low, high, most):
    dual, grad_x, grad_y = b.dual.at[k + 1], b.grad_x.at[k], b.grad_y.at[k]
    half, flux_dx, flux_y = b.dual_half.at[k], b.flux_dx.at[k], b.flux_y.at[k]

    def body(r):
        row = pl.ds(r, 1)
        c, n, s = cross_of(dual, r)
        right, left = beside(c)
        half[row] = ((right + left) + (n + s)) - NEAR * c
        right, left = beside(grad_x[row] * c)
        flux_dx[row] = right - left
        flux_y[row] = grad_y[row] * c

    over_rows(low, high, most, body)


def adjoint_second(k, b, low, high, most):
    half, flux_dx, flux_y, dual_next = b.dual_half.at[k], b.flux_dx.at[k], b.flux_y.at[k], b.dual.at[k]

    def body(r):
        c, n, s = cross_of(half, r)
        right, left = beside(c)
        spread = flux_dx[pl.ds(r, 1)] + (flux_y[pl.ds(r + 1, 1)] - flux_y[pl.ds(r - 1, 1)])
        dual_next[pl.ds(r, 1)] = (((right + left) + (n + s)) - FAR * c) - spread

    over_rows(low, high, most, body)


def by_rows(count, body):
    lax.fori_loop(0, count, lambda i, carry: (body(i), carry)[1], 0)


def spread_tile(tile, dest, first, scale=None):
    def body(i):
        for q in range(4):
            part = tile[pl.ds(q * 8 + i, 8, 32), :]
            dest[OFF + first + i, q * 8 : q * 8 + 8, :] = part if scale is None else part * scale

    by_rows(8, body)


class Buffers:
    def __init__(self, names, refs):
        self.__dict__.update(zip(names, refs, strict=True))


def row_buffer(*lead):
    return pltpu.VMEM((*lead, CHUNKS, LANES), jnp.float32)


def tiles(*lead):
    return pltpu.VMEM((*lead, 8 * CHUNKS, LANES), jnp.float32)


ENDS = ((14, 4), (10, 4), (18, 4), (8, 2), (22, 2), (0, 8), (24, 8))
BACK = ((8, 4), (20, 4), (12, 8))

SCRATCH = {
    "base_in": tiles(4),
    "dir_in": tiles(4),
    "out_tiles": tiles(4),
    "halo_base": tiles(2, 2),
    "halo_dir": tiles(2),
    "next_tiles": tiles(2),
    "next_rows": row_buffer(HELD),
    "prev_ends": row_buffer(HELD),
    "state": row_buffer(STEPS, HELD),
    "state_half": row_buffer(STEPS, HELD),
    "grad_x": row_buffer(STEPS, HELD),
    "grad_y": row_buffer(STEPS, HELD),
    "pert": row_buffer(STEPS + 1, HELD),
    "pert_half": row_buffer(STEPS, HELD),
    "cross": row_buffer(STEPS, HELD),
    "dual": row_buffer(STEPS + 1, HELD),
    "dual_half": row_buffer(STEPS, HELD),
    "flux_dx": row_buffer(STEPS, HELD),
    "flux_y": row_buffer(STEPS, HELD),
    "damp": row_buffer(4),
    "levels": pltpu.VMEM((4, CHUNKS), jnp.int32),
    "table": pltpu.SMEM((4,), jnp.float32),
    "local_sem": pltpu.SemaphoreType.DMA((12,)),
    "halo_send": pltpu.SemaphoreType.DMA((6,)),
    "halo_recv": pltpu.SemaphoreType.DMA((6,)),
    "back_send": pltpu.SemaphoreType.DMA((2 + len(BACK),)),
    "back_recv": pltpu.SemaphoreType.DMA((2 + len(BACK),)),
    "dual_send": pltpu.SemaphoreType.DMA((2,)),
    "dual_recv": pltpu.SemaphoreType.DMA((2,)),
    "ends_send": pltpu.SemaphoreType.DMA((len(ENDS),)),
    "ends_recv": pltpu.SemaphoreType.DMA((len(ENDS),)),
}


def kernel(segments, slabs, base, direction, levels, table, product, *scratch):
    b = Buffers(SCRATCH, scratch)
    tm, sp = lax.axis_index("tm"), lax.axis_index("space")
    after, before = lax.rem(tm + 1, segments), lax.rem(tm + segments - 1, segments)
    below, above = lax.rem(sp + 1, slabs), lax.rem(sp + slabs - 1, slabs)
    next_dev, prev_dev, down_dev, up_dev = (after, sp), (before, sp), (tm, below), (tm, above)

    barrier = pltpu.get_barrier_semaphore()
    for dev in (next_dev, prev_dev, down_dev, up_dev):
        pl.semaphore_signal(barrier, inc=1, device_id=dev, device_id_type=MESH)

    load = [
        pltpu.make_async_copy(base, b.base_in, b.local_sem.at[0]),
        pltpu.make_async_copy(direction, b.dir_in, b.local_sem.at[1]),
        pltpu.make_async_copy(levels, b.levels, b.local_sem.at[2]),
        pltpu.make_async_copy(table, b.table, b.local_sem.at[3]),
    ]
    for copy in load:
        copy.start()

    def remote(src, dst, send, recv, dev):
        return pltpu.make_async_remote_copy(
            src_ref=src, dst_ref=dst, send_sem=send, recv_sem=recv, device_id=dev, device_id_type=MESH
        )

    halo = [
        remote(src, dst, b.halo_send.at[i], b.halo_recv.at[i], dev)
        for i, (src, dst, dev) in enumerate(
            [
                (base.at[3], b.halo_base.at[0, 0], down_dev),
                (base.at[0], b.halo_base.at[1, 0], up_dev),
                (direction.at[3], b.halo_dir.at[0], down_dev),
                (direction.at[0], b.halo_dir.at[1], up_dev),
                (base.at[2], b.halo_base.at[0, 1], down_dev),
                (base.at[1], b.halo_base.at[1, 1], up_dev),
            ]
        )
    ]
    back = [
        remote(direction.at[3 * i], b.next_tiles.at[i], b.back_send.at[i], b.back_recv.at[i], prev_dev)
        for i in range(2)
    ]
    for i, (first, count) in enumerate(BACK):
        rows = pl.ds(OFF + first, count)
        back.append(
            remote(
                b.pert.at[0, rows], b.next_rows.at[rows], b.back_send.at[2 + i], b.back_recv.at[2 + i], prev_dev
            )
        )
    ends = []
    for i, (first, count) in enumerate(ENDS):
        rows = pl.ds(OFF + first, count)
        ends.append(
            remote(b.pert.at[STEPS, rows], b.prev_ends.at[rows], b.ends_send.at[i], b.ends_recv.at[i], next_dev)
        )
    dual = [
        remote(
            b.dual.at[STEPS, pl.ds(OFF + src, 8)],
            b.dual.at[STEPS, pl.ds(OFF + dst, 8)],
            b.dual_send.at[i],
            b.dual_recv.at[i],
            dev,
        )
        for i, (src, dst, dev) in enumerate(((ROWS - 8, -8, down_dev), (0, ROWS, up_dev)))
    ]

    pl.semaphore_wait(barrier, 4)
    for copy in halo[:4]:
        copy.start()
    for copy in back[:2]:
        copy.start()
    for copy in halo[4:]:
        copy.start()

    load[1].wait()
    for t in range(4):
        spread_tile(b.dir_in.at[t], b.pert.at[0], 8 * t)
    for copy in back[2:]:
        copy.start()
    load[0].wait()
    for t in range(4):
        spread_tile(b.base_in.at[t], b.state.at[0], 8 * t, SLOPE)

    def strip(k, low, high, sides, most):
        first_low = low - 1 if sides <= 0 else low + 1
        first_high = high + 1 if sides >= 0 else high - 1
        forward_first(k, b, first_low, first_high, most, base=k < STEPS - 1)
        forward_second(k, b, low, high, most, base=k < STEPS - 1)

    for k in range(STEPS):
        reach = 2 * (STEPS - 1 - k)
        strip(k, 14 - reach, 17 + reach, 0, 32)
    ends[0].start()
    for k in range(STEPS):
        reach = 2 * (STEPS - 1 - k)
        strip(k, 10 - reach, 13 - reach, -1, 32)
        strip(k, 18 + reach, 21 + reach, 1, 32)
    ends[1].start()
    ends[2].start()
    for k in range(STEPS):
        reach = 2 * (STEPS - 1 - k)
        strip(k, 8 - reach, 9 - reach, -1, 32)
        strip(k, 22 + reach, 23 + reach, 1, 32)
    ends[3].start()
    ends[4].start()

    for copy in halo[:4]:
        copy.wait()
    for side, first in ((0, -8), (1, ROWS)):
        spread_tile(b.halo_base.at[side, 0], b.state.at[0], first, SLOPE)
        spread_tile(b.halo_dir.at[side], b.pert.at[0], first)
    for k in range(STEPS):
        strip(k, -6 + 2 * k, 1 + 2 * k, -1, 8)
        strip(k, 30 - 2 * k, 37 - 2 * k, 1, 8)
    ends[5].start()
    ends[6].start()

    for copy in halo[4:]:
        copy.wait()
    for side, first in ((0, -16), (1, ROWS + 8)):
        spread_tile(b.halo_base.at[side, 1], b.state.at[0], first, SLOPE)
    for k in range(STEPS):
        last = k == STEPS - 1
        forward_first(k, b, -15 + 2 * k, -8 + 2 * k, 8, base=not last, tangent=False)
        forward_first(k, b, 39 - 2 * k, 46 - 2 * k, 8, base=not last, tangent=False)
        if not last:
            forward_second(k, b, -14 + 2 * k, -7 + 2 * k, 8, tangent=False)
            forward_second(k, b, 38 - 2 * k, 45 - 2 * k, 8, tangent=False)

    load[2].wait()
    load[3].wait()
    held = b.levels[...]
    coarse = jnp.zeros(held.shape, jnp.float32)
    for level in range(4):
        coarse = coarse + jnp.where(held == level, b.table[level], 0.0)
    entry = lax.broadcasted_iota(jnp.int32, (CHUNKS, CHUNKS), 0)
    chunk = lax.broadcasted_iota(jnp.int32, (CHUNKS, CHUNKS), 1)
    own = chunk == 4 * (entry % 8) + entry // 8
    for t in range(4):
        value = jnp.sum(jnp.where(own, coarse[t : t + 1], 0.0), axis=1, keepdims=True)
        b.damp[t] = jnp.broadcast_to(value, (CHUNKS, LANES))

    def residual(first, count, source):
        def body(i):
            r = OFF + first + i
            b.dual[STEPS, r] = b.pert[STEPS, r] * SCALE - source(r, i)

        by_rows(count, body)

    for side in range(2):
        back[side].wait()
        spread_tile(b.next_tiles.at[side], b.next_rows, 24 * side)
        residual(24 * side, 8, lambda r, i: b.next_rows[r])
    dual[0].start()
    dual[1].start()
    for i in range(2):
        back[2 + i].wait()
        residual(*BACK[i], lambda r, i: b.next_rows[r])
    dual[0].wait()
    dual[1].wait()

    for k in range(STEPS - 1, -1, -1):
        far, near = -2 * k, 3 + 2 * k
        adjoint_first(k, b, far - 1, near + 1, 8)
        adjoint_first(k, b, 30 - near, 32 - far, 8)
        adjoint_second(k, b, far, near, 8)
        adjoint_second(k, b, 31 - near, 31 - far, 8)
    back[4].wait()
    residual(*BACK[2], lambda r, i: b.next_rows[r])
    for k in range(STEPS - 1, -1, -1):
        near = 3 + 2 * k
        adjoint_first(k, b, near + 2, 29 - near, 32)
        adjoint_second(k, b, near + 1, 30 - near, 32)

    def finish(t):
        def body(i):
            r = OFF + 8 * t + i
            value = (b.dual[0, r] - b.prev_ends[r]) * SCALE + (1.0 + b.damp[t]) * b.pert[0, r]
            for q in range(4):
                b.out_tiles[t, pl.ds(q * 8 + i, 8, 32), :] = value[q * 8 : q * 8 + 8]

        by_rows(8, body)
        return pltpu.make_async_copy(b.out_tiles.at[t], product.at[t], b.local_sem.at[4 + t])

    for copy in ends[:5]:
        copy.wait()
    stores = []
    for t in (1, 2, 0, 3):
        if t in (0, 3):
            ends[5 + t // 3].wait()
        stores.append(finish(t))
        stores[-1].start()
    for copy in halo + back + dual:
        pass
    for copy in stores:
        copy.wait()


def as_tiles(shard):
    split = shard.reshape(ROWS // 8, 8, CHUNKS, LANES)
    return split.transpose(0, 2, 1, 3).reshape(ROWS // 8, 8 * CHUNKS, LANES)


def solution(mesh):
    segments, slabs = mesh.shape["tm"], mesh.shape["space"]

    def shards(base_start, direction, damp_levels, damp_table):
        any_spec = pl.BlockSpec(memory_space=pl.ANY)
        result = pl.pallas_call(
            functools.partial(kernel, segments, slabs),
            out_shape=jax.ShapeDtypeStruct((ROWS // 8, 8 * CHUNKS, LANES), jnp.float32),
            in_specs=[any_spec] * 4,
            out_specs=any_spec,
            scratch_shapes=list(SCRATCH.values()),
            compiler_params=pltpu.CompilerParams(
                collective_id=0, has_side_effects=True, vmem_limit_bytes=60 * 2**20
            ),
        )(as_tiles(base_start), as_tiles(direction), damp_levels, damp_table)
        split = result.reshape(ROWS // 8, CHUNKS, 8, LANES).transpose(0, 2, 1, 3)
        return split.reshape(1, ROWS, COLS)

    in_specs = (P("tm", "space", None), P("tm", "space", None), P("space", None), P())
    out_specs = P("tm", "space", None)
    return jax.shard_map(shards, mesh=mesh, in_specs=in_specs, out_specs=out_specs, check_vma=False)
```

time: 91.7 us -> 30.8 us (0.34)
  waiting for transfers between devices: 45.5 us -> 0 us
  Pallas kernels: 0 us -> 28.4 us
  starting transfers between devices: 21.2 us -> 0 us
  other arithmetic: 13.8 us -> 0 us
  local copies, waits for them, and re-layouts: 10.6 us -> 1.87 us
    ppermute x18 -> x0, waiting for transfers between devices: 45.5 us -> none  [the longest x8 21.1 us: with_halo(): after = lax.ppermute(leading, axis, down)]
    pallas_call x0 -> x1, Pallas kernels: none -> 28.4 us  [shards(): pl.pallas_call(functools.partial(kernel, segments, slabs), out_shape=jax....]
    ppermute x18 -> x0, starting transfers between devices: 21.2 us -> none  [the longest x8 14.8 us: with_halo(): before = lax.ppermute(last, axis, up)]
    slice x57 -> x0, local copies, waits for them, and re-layouts: 8.2 us -> none  [the longest x32 5.22 us: laplace(): jnp.roll(center, -1, -1)]
    sub x10 -> x0, other arithmetic: 5.74 us -> none  [the longest x3 2.18 us: tangent_step(): shave(pert_pad, 2) - coef_lap * shave(first, 1) - coef_bih * second]
    mul x7 -> x0, other arithmetic: 2.15 us -> none  [the longest x4 1.55 us: adjoint_step(): flux_x = slope_cols(base_pad) * inner]
    broadcast_in_dim x1 -> x0, other arithmetic: 1.62 us -> none  [shards(): return result[None]]
    concatenate x11 -> x0, other arithmetic: 1.55 us -> none  [with_halo(): shard = jnp.concatenate([before, shard, after], axis=dim)]
  transfers between devices with their start and end apart: 18 -> 0, of which waited for: 14 -> 0; matrix products, arithmetic and copies ran while one was open for 4% -> 0% of each run, Pallas kernels for 0% -> 0%
where the time goes in v1:
time: 30.8 us; the launch traced here: 30.3 us
  Pallas kernels  28.4 us (92%)
  local copies, waits for them, and re-layouts  1.87 us (6%)
    pallas_call x1, Pallas kernels, shards(): pl.pallas_call(functools.partial(kernel, segments, slabs), out_shape=jax....  28.4 us
    unnamed x1, local copies, waits for them, and re-layouts  1.87 us

profile of v1, /device:TPU:97, one launch (start us, length us, event | category | flops | bytes accessed | tf_op | source)
XLA Modules:
  0.0 30.3 jit_solution(3003678680059663943)
XLA Ops:
  0.0 28.4 %shard_map.46 = f32[4,256,128]{2,1,0:T(8,128)} custom-call(f32[4,256,128]{2,1,0:T(8,128)} %bitcast.16, f32[4,256,128]{2,1,0:T(8,128)} %bitcast.17, s32[4,32]{1,0:T(4,128)} %levels.1, f32[4]{0:T(128)} %table.1), custom_call_target="tpu_custom_call" | custom-call | tf_op jit(solution)/shard_map/pallas_call | solution.py:409
  28.4 1.9 %copy.6 = f32[1,32,4096]{2,1,0:T(8,128)} copy(f32[1,32,4096]{2,1,0:T(8,128)} %bitcast.15) | data formatting | bytes 1048576

commit v2 on v1

--- a/solution.py
+++ b/solution.py
@@ -31,14 +31,30 @@
 
 def beside(x):
     lane = lax.broadcasted_iota(jnp.int32, (1, 1, LANES), 2)
-    right = pltpu.roll(x, LANES - 1, 2)
-    left = pltpu.roll(x, 1, 2)
-    right_next = jnp.concatenate([right[:, 8:], pltpu.roll(right[:, :8], 7, 1)], 1)
-    left_next = jnp.concatenate([pltpu.roll(left[:, 24:], 1, 1), left[:, :24]], 1)
-    return (
-        jnp.where(lane == LANES - 1, right_next, right),
-        jnp.where(lane == 0, left_next, left),
-    )
+    turned = pltpu.roll(x[:, :8], LANES - 1, 2)
+    last = jnp.where(lane == LANES - 1, pltpu.roll(turned, 7, 1), turned)
+    turned = pltpu.roll(x[:, 24:], 1, 2)
+    first = jnp.where(lane == 0, pltpu.roll(turned, 1, 1), turned)
+    return jnp.concatenate([x[:, 8:], last], 1), jnp.concatenate([first, x[:, :24]], 1)
+
+
+def permute(parts, order):
+    x = jnp.concatenate(parts, 1)
+    high = x.astype(jnp.bfloat16)
+    rest = x - high.astype(jnp.float32)
+    middle = rest.astype(jnp.bfloat16)
+    low = (rest - middle.astype(jnp.float32)).astype(jnp.bfloat16)
+    n = x.shape[0]
+    out = jnp.dot(jnp.concatenate([high, middle, low], 0), order, preferred_element_type=jnp.float32)
+    return (out[:n] + out[n : 2 * n]) + out[2 * n :]
+
+
+def fill_orders(forth, back):
+    for ref, source, target in ((forth, 0, 1), (back, 1, 0)):
+        cell = lax.broadcasted_iota(jnp.int32, ref.shape, source)
+        entry = lax.broadcasted_iota(jnp.int32, ref.shape, target)
+        hit = cell == (entry % LANES) * 4 + entry // LANES
+        ref[...] = jnp.where(hit, 1.0, 0.0).astype(jnp.bfloat16)
 
 
 def over_rows(low, high, most, body):
@@ -138,13 +154,15 @@
     lax.fori_loop(0, count, lambda i, carry: (body(i), carry)[1], 0)
 
 
-def spread_tile(tile, dest, first, scale=None):
-    def body(i):
-        for q in range(4):
-            part = tile[pl.ds(q * 8 + i, 8, 32), :]
-            dest[OFF + first + i, q * 8 : q * 8 + 8, :] = part if scale is None else part * scale
-
-    by_rows(8, body)
+def interleave(tiles_in, order, dest, scale=None):
+    parts = []
+    for a in range(4):
+        pieces = [tiles_in[t, pl.ds(a * 8 + i, 8, 32), :] for t in range(4) for i in range(8)]
+        parts.append(jnp.concatenate(pieces, 0))
+    out = permute(parts, order[...])
+    for q in range(4):
+        part = out[:, q * LANES : (q + 1) * LANES].reshape(ROWS, 8, LANES)
+        dest[OFF : OFF + ROWS, q * 8 : q * 8 + 8, :] = part if scale is None else part * scale
 
 
 class Buffers:
@@ -161,15 +179,22 @@
 
 
 ENDS = ((14, 4), (10, 4), (18, 4), (8, 2), (22, 2), (0, 8), (24, 8))
-BACK = ((8, 4), (20, 4), (12, 8))
+BACK = ((0, 8), (24, 8), (8, 4), (20, 4), (12, 8))
+HALO = (
+    (True, 24, -8, True),
+    (True, 0, 32, False),
+    (False, 24, -8, True),
+    (False, 0, 32, False),
+    (False, 16, -16, True),
+    (False, 8, 40, False),
+)
 
 SCRATCH = {
     "base_in": tiles(4),
     "dir_in": tiles(4),
     "out_tiles": tiles(4),
-    "halo_base": tiles(2, 2),
-    "halo_dir": tiles(2),
-    "next_tiles": tiles(2),
+    "forth": pltpu.VMEM((4 * LANES, 4 * LANES), jnp.bfloat16),
+    "back": pltpu.VMEM((4 * LANES, 4 * LANES), jnp.bfloat16),
     "next_rows": row_buffer(HELD),
     "prev_ends": row_buffer(HELD),
     "state": row_buffer(STEPS, HELD),
@@ -183,14 +208,14 @@
     "dual_half": row_buffer(STEPS, HELD),
     "flux_dx": row_buffer(STEPS, HELD),
     "flux_y": row_buffer(STEPS, HELD),
-    "damp": row_buffer(4),
+    "damp": pltpu.VMEM((4, 8, LANES), jnp.float32),
     "levels": pltpu.VMEM((4, CHUNKS), jnp.int32),
     "table": pltpu.SMEM((4,), jnp.float32),
     "local_sem": pltpu.SemaphoreType.DMA((12,)),
-    "halo_send": pltpu.SemaphoreType.DMA((6,)),
-    "halo_recv": pltpu.SemaphoreType.DMA((6,)),
-    "back_send": pltpu.SemaphoreType.DMA((2 + len(BACK),)),
-    "back_recv": pltpu.SemaphoreType.DMA((2 + len(BACK),)),
+    "halo_send": pltpu.SemaphoreType.DMA((len(HALO),)),
+    "halo_recv": pltpu.SemaphoreType.DMA((len(HALO),)),
+    "back_send": pltpu.SemaphoreType.DMA((len(BACK),)),
+    "back_recv": pltpu.SemaphoreType.DMA((len(BACK),)),
     "dual_send": pltpu.SemaphoreType.DMA((2,)),
     "dual_recv": pltpu.SemaphoreType.DMA((2,)),
     "ends_send": pltpu.SemaphoreType.DMA((len(ENDS),)),
@@ -223,30 +248,22 @@
             src_ref=src, dst_ref=dst, send_sem=send, recv_sem=recv, device_id=dev, device_id_type=MESH
         )
 
-    halo = [
-        remote(src, dst, b.halo_send.at[i], b.halo_recv.at[i], dev)
-        for i, (src, dst, dev) in enumerate(
-            [
-                (base.at[3], b.halo_base.at[0, 0], down_dev),
-                (base.at[0], b.halo_base.at[1, 0], up_dev),
-                (direction.at[3], b.halo_dir.at[0], down_dev),
-                (direction.at[0], b.halo_dir.at[1], up_dev),
-                (base.at[2], b.halo_base.at[0, 1], down_dev),
-                (base.at[1], b.halo_base.at[1, 1], up_dev),
-            ]
+    halo = []
+    for i, (is_dir, src, dst, down) in enumerate(HALO):
+        held = (b.pert if is_dir else b.state).at[0]
+        halo.append(
+            remote(
+                held.at[pl.ds(OFF + src, 8)],
+                held.at[pl.ds(OFF + dst, 8)],
+                b.halo_send.at[i],
+                b.halo_recv.at[i],
+                down_dev if down else up_dev,
+            )
         )
-    ]
-    back = [
-        remote(direction.at[3 * i], b.next_tiles.at[i], b.back_send.at[i], b.back_recv.at[i], prev_dev)
-        for i in range(2)
-    ]
+    back = []
     for i, (first, count) in enumerate(BACK):
         rows = pl.ds(OFF + first, count)
-        back.append(
-            remote(
-                b.pert.at[0, rows], b.next_rows.at[rows], b.back_send.at[2 + i], b.back_recv.at[2 + i], prev_dev
-            )
-        )
+        back.append(remote(b.pert.at[0, rows], b.next_rows.at[rows], b.back_send.at[i], b.back_recv.at[i], prev_dev))
     ends = []
     for i, (first, count) in enumerate(ENDS):
         rows = pl.ds(OFF + first, count)
@@ -261,25 +278,19 @@
             b.dual_recv.at[i],
             dev,
         )
-        for i, (src, dst, dev) in enumerate(((ROWS - 8, -8, down_dev), (0, ROWS, up_dev)))
+        for i, (src, dst, dev) in enumerate(((0, ROWS, up_dev), (ROWS - 8, -8, down_dev)))
     ]
 
+    fill_orders(b.forth, b.back)
+    load[1].wait()
+    interleave(b.dir_in, b.forth, b.pert.at[0])
     pl.semaphore_wait(barrier, 4)
-    for copy in halo[:4]:
-        copy.start()
-    for copy in back[:2]:
-        copy.start()
-    for copy in halo[4:]:
-        copy.start()
-
-    load[1].wait()
-    for t in range(4):
-        spread_tile(b.dir_in.at[t], b.pert.at[0], 8 * t)
-    for copy in back[2:]:
+    for copy in back[:2] + halo[:2] + back[2:]:
         copy.start()
     load[0].wait()
-    for t in range(4):
-        spread_tile(b.base_in.at[t], b.state.at[0], 8 * t, SLOPE)
+    interleave(b.base_in, b.forth, b.state.at[0], SLOPE)
+    for copy in halo[2:]:
+        copy.start()
 
     def strip(k, low, high, sides, most):
         first_low = low - 1 if sides <= 0 else low + 1
@@ -306,9 +317,6 @@
 
     for copy in halo[:4]:
         copy.wait()
-    for side, first in ((0, -8), (1, ROWS)):
-        spread_tile(b.halo_base.at[side, 0], b.state.at[0], first, SLOPE)
-        spread_tile(b.halo_dir.at[side], b.pert.at[0], first)
     for k in range(STEPS):
         strip(k, -6 + 2 * k, 1 + 2 * k, -1, 8)
         strip(k, 30 - 2 * k, 37 - 2 * k, 1, 8)
@@ -317,8 +325,6 @@
 
     for copy in halo[4:]:
         copy.wait()
-    for side, first in ((0, -16), (1, ROWS + 8)):
-        spread_tile(b.halo_base.at[side, 1], b.state.at[0], first, SLOPE)
     for k in range(STEPS):
         last = k == STEPS - 1
         forward_first(k, b, -15 + 2 * k, -8 + 2 * k, 8, base=not last, tangent=False)
@@ -333,29 +339,27 @@
     coarse = jnp.zeros(held.shape, jnp.float32)
     for level in range(4):
         coarse = coarse + jnp.where(held == level, b.table[level], 0.0)
-    entry = lax.broadcasted_iota(jnp.int32, (CHUNKS, CHUNKS), 0)
-    chunk = lax.broadcasted_iota(jnp.int32, (CHUNKS, CHUNKS), 1)
-    own = chunk == 4 * (entry % 8) + entry // 8
+    entry = lax.broadcasted_iota(jnp.int32, (8, CHUNKS), 0)
+    chunk = lax.broadcasted_iota(jnp.int32, (8, CHUNKS), 1)
+    quarter = lax.broadcasted_iota(jnp.int32, (8, LANES), 1) // 32
     for t in range(4):
-        value = jnp.sum(jnp.where(own, coarse[t : t + 1], 0.0), axis=1, keepdims=True)
-        b.damp[t] = jnp.broadcast_to(value, (CHUNKS, LANES))
-
-    def residual(first, count, source):
-        def body(i):
-            r = OFF + first + i
-            b.dual[STEPS, r] = b.pert[STEPS, r] * SCALE - source(r, i)
-
-        by_rows(count, body)
+        value = jnp.zeros((8, LANES), jnp.float32)
+        for a in range(4):
+            own = jnp.where(chunk == 4 * entry + a, coarse[t : t + 1], 0.0)
+            value = value + jnp.where(quarter == a, jnp.sum(own, axis=1, keepdims=True), 0.0)
+        b.damp[t] = value
+
+    def residual(first, count):
+        rows = pl.ds(OFF + first, count)
+        b.dual[STEPS, rows] = b.pert[STEPS, rows] * SCALE - b.next_rows[rows]
 
     for side in range(2):
         back[side].wait()
-        spread_tile(b.next_tiles.at[side], b.next_rows, 24 * side)
-        residual(24 * side, 8, lambda r, i: b.next_rows[r])
-    dual[0].start()
-    dual[1].start()
-    for i in range(2):
-        back[2 + i].wait()
-        residual(*BACK[i], lambda r, i: b.next_rows[r])
+        residual(*BACK[side])
+        dual[side].start()
+    for i in (2, 3):
+        back[i].wait()
+        residual(*BACK[i])
     dual[0].wait()
     dual[1].wait()
 
@@ -366,32 +370,38 @@
         adjoint_second(k, b, far, near, 8)
         adjoint_second(k, b, 31 - near, 31 - far, 8)
     back[4].wait()
-    residual(*BACK[2], lambda r, i: b.next_rows[r])
+    residual(*BACK[4])
     for k in range(STEPS - 1, -1, -1):
         near = 3 + 2 * k
         adjoint_first(k, b, near + 2, 29 - near, 32)
         adjoint_second(k, b, near + 1, 30 - near, 32)
 
-    def finish(t):
-        def body(i):
-            r = OFF + 8 * t + i
-            value = (b.dual[0, r] - b.prev_ends[r]) * SCALE + (1.0 + b.damp[t]) * b.pert[0, r]
-            for q in range(4):
-                b.out_tiles[t, pl.ds(q * 8 + i, 8, 32), :] = value[q * 8 : q * 8 + 8]
-
-        by_rows(8, body)
-        return pltpu.make_async_copy(b.out_tiles.at[t], product.at[t], b.local_sem.at[4 + t])
+    def finish(tiles_done):
+        parts = [[] for _ in range(4)]
+        for t in tiles_done:
+            scaled = 1.0 + jnp.concatenate([b.damp[t]] * 4, 0)
+            for i in range(8):
+                r = OFF + 8 * t + i
+                value = (b.dual[0, r] - b.prev_ends[r]) * SCALE + scaled * b.pert[0, r]
+                for q in range(4):
+                    parts[q].append(value[8 * q : 8 * q + 8])
+        out = permute([jnp.concatenate(part, 0) for part in parts], b.back[...])
+        stores = []
+        for j, t in enumerate(tiles_done):
+            for i in range(8):
+                for a in range(4):
+                    value = out[64 * j + 8 * i : 64 * j + 8 * i + 8, a * LANES : (a + 1) * LANES]
+                    b.out_tiles[t, pl.ds(a * 8 + i, 8, 32), :] = value
+            stores.append(pltpu.make_async_copy(b.out_tiles.at[t], product.at[t], b.local_sem.at[4 + t]))
+            stores[-1].start()
+        return stores
 
     for copy in ends[:5]:
         copy.wait()
-    stores = []
-    for t in (1, 2, 0, 3):
-        if t in (0, 3):
-            ends[5 + t // 3].wait()
-        stores.append(finish(t))
-        stores[-1].start()
-    for copy in halo + back + dual:
-        pass
+    stores = finish((1, 2))
+    for copy in ends[5:]:
+        copy.wait()
+    stores += finish((0, 3))
     for copy in stores:
         copy.wait()
 

time: 30.8 us -> 26.2 us (0.85)
  the two profiles are of different devices: /device:TPU:97 before, /device:TPU:1 now
where the time goes in v2:
time: 26.2 us; the launch traced here: 26.1 us
  Pallas kernels  24.2 us (92%)
  local copies, waits for them, and re-layouts  1.87 us (7%)
    pallas_call x1, Pallas kernels, shards(): pl.pallas_call(functools.partial(kernel, segments, slabs), out_shape=jax....  24.2 us
    unnamed x1, local copies, waits for them, and re-layouts  1.87 us

profile of v2, /device:TPU:1, one launch (start us, length us, event | category | flops | bytes accessed | tf_op | source)
XLA Modules:
  0.0 26.1 jit_solution(16000228912910159977)
XLA Ops:
  0.0 24.2 %shard_map.46 = f32[4,256,128]{2,1,0:T(8,128)} custom-call(f32[4,256,128]{2,1,0:T(8,128)} %bitcast.16, f32[4,256,128]{2,1,0:T(8,128)} %bitcast.17, s32[4,32]{1,0:T(4,128)} %levels.1, f32[4]{0:T(128)} %table.1), custom_call_target="tpu_custom_call" | custom-call | tf_op jit(solution)/shard_map/pallas_call | solution.py:419
  24.2 1.9 %copy.6 = f32[1,32,4096]{2,1,0:T(8,128)} copy(f32[1,32,4096]{2,1,0:T(8,128)} %bitcast.15) | data formatting | bytes 1048576

commit v3 on v2

--- a/solution.py
+++ b/solution.py
@@ -49,12 +49,10 @@
     return (out[:n] + out[n : 2 * n]) + out[2 * n :]
 
 
-def fill_orders(forth, back):
-    for ref, source, target in ((forth, 0, 1), (back, 1, 0)):
-        cell = lax.broadcasted_iota(jnp.int32, ref.shape, source)
-        entry = lax.broadcasted_iota(jnp.int32, ref.shape, target)
-        hit = cell == (entry % LANES) * 4 + entry // LANES
-        ref[...] = jnp.where(hit, 1.0, 0.0).astype(jnp.bfloat16)
+def order_of(shape, forth):
+    cell = lax.broadcasted_iota(jnp.int32, shape, 0 if forth else 1)
+    entry = lax.broadcasted_iota(jnp.int32, shape, 1 if forth else 0)
+    return jnp.where(cell == (entry % LANES) * 4 + entry // LANES, 1.0, 0.0).astype(jnp.bfloat16)
 
 
 def over_rows(low, high, most, body):
@@ -154,15 +152,16 @@
     lax.fori_loop(0, count, lambda i, carry: (body(i), carry)[1], 0)
 
 
-def interleave(tiles_in, order, dest, scale=None):
+def interleave(slabs_in, order, dests, scales):
     parts = []
     for a in range(4):
-        pieces = [tiles_in[t, pl.ds(a * 8 + i, 8, 32), :] for t in range(4) for i in range(8)]
+        pieces = [slab[t, pl.ds(a * 8 + i, 8, 32), :] for slab in slabs_in for t in range(4) for i in range(8)]
         parts.append(jnp.concatenate(pieces, 0))
     out = permute(parts, order[...])
-    for q in range(4):
-        part = out[:, q * LANES : (q + 1) * LANES].reshape(ROWS, 8, LANES)
-        dest[OFF : OFF + ROWS, q * 8 : q * 8 + 8, :] = part if scale is None else part * scale
+    for j, (dest, scale) in enumerate(zip(dests, scales, strict=True)):
+        for q in range(4):
+            part = out[j * ROWS * 8 : (j + 1) * ROWS * 8, q * LANES : (q + 1) * LANES].reshape(ROWS, 8, LANES)
+            dest[OFF : OFF + ROWS, q * 8 : q * 8 + 8, :] = part if scale is None else part * scale
 
 
 class Buffers:
@@ -192,7 +191,6 @@
 SCRATCH = {
     "base_in": tiles(4),
     "dir_in": tiles(4),
-    "out_tiles": tiles(4),
     "forth": pltpu.VMEM((4 * LANES, 4 * LANES), jnp.bfloat16),
     "back": pltpu.VMEM((4 * LANES, 4 * LANES), jnp.bfloat16),
     "next_rows": row_buffer(HELD),
@@ -281,15 +279,12 @@
         for i, (src, dst, dev) in enumerate(((0, ROWS, up_dev), (ROWS - 8, -8, down_dev)))
     ]
 
-    fill_orders(b.forth, b.back)
+    b.forth[...] = order_of(b.forth.shape, True)
     load[1].wait()
-    interleave(b.dir_in, b.forth, b.pert.at[0])
+    load[0].wait()
+    interleave([b.dir_in, b.base_in], b.forth, [b.pert.at[0], b.state.at[0]], [None, SLOPE])
     pl.semaphore_wait(barrier, 4)
-    for copy in back[:2] + halo[:2] + back[2:]:
-        copy.start()
-    load[0].wait()
-    interleave(b.base_in, b.forth, b.state.at[0], SLOPE)
-    for copy in halo[2:]:
+    for copy in halo[:2] + back[:1] + halo[2:4] + back[1:] + halo[4:]:
         copy.start()
 
     def strip(k, low, high, sides, most):
@@ -315,6 +310,7 @@
     ends[3].start()
     ends[4].start()
 
+    b.back[...] = order_of(b.back.shape, False)
     for copy in halo[:4]:
         copy.wait()
     for k in range(STEPS):
@@ -323,6 +319,14 @@
     ends[5].start()
     ends[6].start()
 
+    def residual(first, count):
+        rows = pl.ds(OFF + first, count)
+        b.dual[STEPS, rows] = b.pert[STEPS, rows] * SCALE - b.next_rows[rows]
+
+    for side in range(2):
+        back[side].wait()
+        residual(*BACK[side])
+        dual[side].start()
     for copy in halo[4:]:
         copy.wait()
     for k in range(STEPS):
@@ -349,14 +353,6 @@
             value = value + jnp.where(quarter == a, jnp.sum(own, axis=1, keepdims=True), 0.0)
         b.damp[t] = value
 
-    def residual(first, count):
-        rows = pl.ds(OFF + first, count)
-        b.dual[STEPS, rows] = b.pert[STEPS, rows] * SCALE - b.next_rows[rows]
-
-    for side in range(2):
-        back[side].wait()
-        residual(*BACK[side])
-        dual[side].start()
     for i in (2, 3):
         back[i].wait()
         residual(*BACK[i])
@@ -386,24 +382,18 @@
                 for q in range(4):
                     parts[q].append(value[8 * q : 8 * q + 8])
         out = permute([jnp.concatenate(part, 0) for part in parts], b.back[...])
-        stores = []
         for j, t in enumerate(tiles_done):
             for i in range(8):
                 for a in range(4):
                     value = out[64 * j + 8 * i : 64 * j + 8 * i + 8, a * LANES : (a + 1) * LANES]
-                    b.out_tiles[t, pl.ds(a * 8 + i, 8, 32), :] = value
-            stores.append(pltpu.make_async_copy(b.out_tiles.at[t], product.at[t], b.local_sem.at[4 + t]))
-            stores[-1].start()
-        return stores
+                    product[t, pl.ds(a * 8 + i, 8, 32), :] = value
 
     for copy in ends[:5]:
         copy.wait()
-    stores = finish((1, 2))
+    finish((1, 2))
     for copy in ends[5:]:
         copy.wait()
-    stores += finish((0, 3))
-    for copy in stores:
-        copy.wait()
+    finish((0, 3))
 
 
 def as_tiles(shard):
@@ -418,12 +408,12 @@
         any_spec = pl.BlockSpec(memory_space=pl.ANY)
         result = pl.pallas_call(
             functools.partial(kernel, segments, slabs),
-            out_shape=jax.ShapeDtypeStruct((ROWS // 8, 8 * CHUNKS, LANES), jnp.float32),
+            out_shape=tiles(4),
             in_specs=[any_spec] * 4,
-            out_specs=any_spec,
+            out_specs=pl.BlockSpec(memory_space=pltpu.VMEM),
             scratch_shapes=list(SCRATCH.values()),
             compiler_params=pltpu.CompilerParams(
-                collective_id=0, has_side_effects=True, vmem_limit_bytes=60 * 2**20
+                collective_id=0, has_side_effects=True, vmem_limit_bytes=56 * 2**20
             ),
         )(as_tiles(base_start), as_tiles(direction), damp_levels, damp_table)
         split = result.reshape(ROWS // 8, CHUNKS, 8, LANES).transpose(0, 2, 1, 3)

time: 26.2 us -> 24.1 us (0.920)
  the two profiles are of different devices: /device:TPU:1 before, /device:TPU:30 now
where the time goes in v3:
time: 24.1 us; the launch traced here: 24 us
  Pallas kernels  23.2 us (96%)
  local copies, waits for them, and re-layouts  0.8 us (3%)
    pallas_call x1, Pallas kernels, shards(): pl.pallas_call(functools.partial(kernel, segments, slabs), out_shape=tile...  23.2 us
    unnamed x1, local copies, waits for them, and re-layouts  0.8 us

profile of v3, /device:TPU:30, one launch (start us, length us, event | category | flops | bytes accessed | tf_op | source)
XLA Modules:
  0.0 24.0 jit_solution(2154381870166091310)
XLA Ops:
  0.0 23.2 %shard_map.46 = f32[4,256,128]{2,1,0:T(8,128)S(1)} custom-call(f32[4,256,128]{2,1,0:T(8,128)} %bitcast.16, f32[4,256,128]{2,1,0:T(8,128)} %bitcast.17, s32[4,32]{1,0:T(4,128)} %levels.1, f32[4]{0:T(128)} %table.1), custom_call_target="tpu_custom_call" | custom-call | tf_op jit(solution)/shard_map/pallas_call | solution.py:409
  23.2 0.8 %copy.6 = f32[1,32,4096]{2,1,0:T(8,128)} copy(f32[1,32,4096]{2,1,0:T(8,128)S(1)} %bitcast.15) | data formatting | bytes 1048576

commit v4 on v3

--- a/solution.py
+++ b/solution.py
@@ -55,8 +55,7 @@
     return jnp.where(cell == (entry % LANES) * 4 + entry // LANES, 1.0, 0.0).astype(jnp.bfloat16)
 
 
-def over_rows(low, high, most, body):
-    count = high - low + 1
+def over_rows(low, count, most, body):
     steps = -(-count // most)
     size = -(-count // steps)
 
@@ -75,7 +74,7 @@
     return ref[pl.ds(r, 1)], ref[pl.ds(r - 1, 1)], ref[pl.ds(r + 1, 1)]
 
 
-def forward_first(k, b, low, high, most, base=True, tangent=True):
+def forward_first(k, b, low, count, most, base=True, tangent=True):
     state, half, grad_x, grad_y = b.state.at[k], b.state_half.at[k], b.grad_x.at[k], b.grad_y.at[k]
     pert, pert_half, cross = b.pert.at[k], b.pert_half.at[k], b.cross.at[k]
 
@@ -94,10 +93,10 @@
             pert_half[row] = ((right + left) + (n + s)) - NEAR * c
             cross[row] = slope_x * (right - left) + slope_y * (s - n)
 
-    over_rows(low, high, most, body)
-
-
-def forward_second(k, b, low, high, most, base=True, tangent=True):
+    over_rows(low, count, most, body)
+
+
+def forward_second(k, b, low, count, most, base=True, tangent=True):
     half, grad_x, grad_y = b.state_half.at[k], b.grad_x.at[k], b.grad_y.at[k]
     pert_half, cross, pert_next = b.pert_half.at[k], b.cross.at[k], b.pert.at[k + 1]
     if base:
@@ -117,10 +116,10 @@
             right, left = beside(c)
             pert_next[row] = (((right + left) + (n + s)) - FAR * c) + cross[row]
 
-    over_rows(low, high, most, body)
-
-
-def adjoint_first(k, b, low, high, most):
+    over_rows(low, count, most, body)
+
+
+def adjoint_first(k, b, low, count, most):
     dual, grad_x, grad_y = b.dual.at[k + 1], b.grad_x.at[k], b.grad_y.at[k]
     half, flux_dx, flux_y = b.dual_half.at[k], b.flux_dx.at[k], b.flux_y.at[k]
 
@@ -133,10 +132,10 @@
         flux_dx[row] = right - left
         flux_y[row] = grad_y[row] * c
 
-    over_rows(low, high, most, body)
-
-
-def adjoint_second(k, b, low, high, most):
+    over_rows(low, count, most, body)
+
+
+def adjoint_second(k, b, low, count, most):
     half, flux_dx, flux_y, dual_next = b.dual_half.at[k], b.flux_dx.at[k], b.flux_y.at[k], b.dual.at[k]
 
     def body(r):
@@ -145,7 +144,7 @@
         spread = flux_dx[pl.ds(r, 1)] + (flux_y[pl.ds(r + 1, 1)] - flux_y[pl.ds(r - 1, 1)])
         dual_next[pl.ds(r, 1)] = (((right + left) + (n + s)) - FAR * c) - spread
 
-    over_rows(low, high, most, body)
+    over_rows(low, count, most, body)
 
 
 def by_rows(count, body):
@@ -227,6 +226,13 @@
     after, before = lax.rem(tm + 1, segments), lax.rem(tm + segments - 1, segments)
     below, above = lax.rem(sp + 1, slabs), lax.rem(sp + slabs - 1, slabs)
     next_dev, prev_dev, down_dev, up_dev = (after, sp), (before, sp), (tm, below), (tm, above)
+    even = lax.rem(sp, 2) == 0
+    lower_first = even | (sp == slabs - 1)
+
+    def back_row(i):
+        first, count = BACK[i]
+        return first if i == 4 else jnp.where(even, first, ROWS - count - first)
+
 
     barrier = pltpu.get_barrier_semaphore()
     for dev in (next_dev, prev_dev, down_dev, up_dev):
@@ -259,8 +265,8 @@
             )
         )
     back = []
-    for i, (first, count) in enumerate(BACK):
-        rows = pl.ds(OFF + first, count)
+    for i, (_, count) in enumerate(BACK):
+        rows = pl.ds(OFF + back_row(i), count)
         back.append(remote(b.pert.at[0, rows], b.next_rows.at[rows], b.back_send.at[i], b.back_recv.at[i], prev_dev))
     ends = []
     for i, (first, count) in enumerate(ENDS):
@@ -268,16 +274,25 @@
         ends.append(
             remote(b.pert.at[STEPS, rows], b.prev_ends.at[rows], b.ends_send.at[i], b.ends_recv.at[i], next_dev)
         )
-    dual = [
-        remote(
-            b.dual.at[STEPS, pl.ds(OFF + src, 8)],
-            b.dual.at[STEPS, pl.ds(OFF + dst, 8)],
-            b.dual_send.at[i],
-            b.dual_recv.at[i],
-            dev,
+    dual = []
+    for i in range(2):
+        down = ~even if i == 0 else even
+        src, dst = jnp.where(down, ROWS - 8, 0), jnp.where(down, -8, ROWS)
+        sem = jnp.where(down, 0, 1)
+        dual.append(
+            remote(
+                b.dual.at[STEPS, pl.ds(OFF + src, 8)],
+                b.dual.at[STEPS, pl.ds(OFF + dst, 8)],
+                b.dual_send.at[sem],
+                b.dual_recv.at[sem],
+                (tm, jnp.where(down, below, above)),
+            )
         )
-        for i, (src, dst, dev) in enumerate(((0, ROWS, up_dev), (ROWS - 8, -8, down_dev)))
-    ]
+
+    def dual_arrived(lower):
+        rows = b.dual.at[STEPS, pl.ds(OFF + jnp.where(lower, ROWS, -8), 8)]
+        sem = jnp.where(lower, 1, 0)
+        remote(rows, rows, b.dual_send.at[sem], b.dual_recv.at[sem], up_dev).wait_recv()
 
     b.forth[...] = order_of(b.forth.shape, True)
     load[1].wait()
@@ -290,8 +305,8 @@
     def strip(k, low, high, sides, most):
         first_low = low - 1 if sides <= 0 else low + 1
         first_high = high + 1 if sides >= 0 else high - 1
-        forward_first(k, b, first_low, first_high, most, base=k < STEPS - 1)
-        forward_second(k, b, low, high, most, base=k < STEPS - 1)
+        forward_first(k, b, first_low, first_high - first_low + 1, most, base=k < STEPS - 1)
+        forward_second(k, b, low, high - low + 1, most, base=k < STEPS - 1)
 
     for k in range(STEPS):
         reach = 2 * (STEPS - 1 - k)
@@ -325,17 +340,17 @@
 
     for side in range(2):
         back[side].wait()
-        residual(*BACK[side])
+        residual(back_row(side), 8)
         dual[side].start()
     for copy in halo[4:]:
         copy.wait()
     for k in range(STEPS):
         last = k == STEPS - 1
-        forward_first(k, b, -15 + 2 * k, -8 + 2 * k, 8, base=not last, tangent=False)
-        forward_first(k, b, 39 - 2 * k, 46 - 2 * k, 8, base=not last, tangent=False)
+        forward_first(k, b, -15 + 2 * k, 8, 8, base=not last, tangent=False)
+        forward_first(k, b, 39 - 2 * k, 8, 8, base=not last, tangent=False)
         if not last:
-            forward_second(k, b, -14 + 2 * k, -7 + 2 * k, 8, tangent=False)
-            forward_second(k, b, 38 - 2 * k, 45 - 2 * k, 8, tangent=False)
+            forward_second(k, b, -14 + 2 * k, 8, 8, tangent=False)
+            forward_second(k, b, 38 - 2 * k, 8, 8, tangent=False)
 
     load[2].wait()
     load[3].wait()
@@ -353,24 +368,21 @@
             value = value + jnp.where(quarter == a, jnp.sum(own, axis=1, keepdims=True), 0.0)
         b.damp[t] = value
 
+    def turned(first, count):
+        return jnp.where(lower_first, first, ROWS - count - first)
+
     for i in (2, 3):
         back[i].wait()
-        residual(*BACK[i])
-    dual[0].wait()
-    dual[1].wait()
-
+        residual(back_row(i), 4)
+    dual_arrived(lower_first)
     for k in range(STEPS - 1, -1, -1):
-        far, near = -2 * k, 3 + 2 * k
-        adjoint_first(k, b, far - 1, near + 1, 8)
-        adjoint_first(k, b, 30 - near, 32 - far, 8)
-        adjoint_second(k, b, far, near, 8)
-        adjoint_second(k, b, 31 - near, 31 - far, 8)
+        adjoint_first(k, b, turned(27 - 2 * k, 6 + 4 * k), 6 + 4 * k, 32)
+        adjoint_second(k, b, turned(28 - 2 * k, 4 + 4 * k), 4 + 4 * k, 32)
     back[4].wait()
     residual(*BACK[4])
     for k in range(STEPS - 1, -1, -1):
-        near = 3 + 2 * k
-        adjoint_first(k, b, near + 2, 29 - near, 32)
-        adjoint_second(k, b, near + 1, 30 - near, 32)
+        adjoint_first(k, b, turned(7 - 2 * k, 20), 20, 32)
+        adjoint_second(k, b, turned(8 - 2 * k, 20), 20, 32)
 
     def finish(tiles_done):
         parts = [[] for _ in range(4)]
@@ -388,6 +400,12 @@
                     value = out[64 * j + 8 * i : 64 * j + 8 * i + 8, a * LANES : (a + 1) * LANES]
                     product[t, pl.ds(a * 8 + i, 8, 32), :] = value
 
+    dual_arrived(~lower_first)
+    for copy in dual:
+        copy.wait_send()
+    for k in range(STEPS - 1, -1, -1):
+        adjoint_first(k, b, turned(-2 * k - 1, 8), 8, 8)
+        adjoint_second(k, b, turned(-2 * k, 8), 8, 8)
     for copy in ends[:5]:
         copy.wait()
     finish((1, 2))

time: 24.1 us -> 23.6 us (0.979)
  the two profiles are of different devices: /device:TPU:30 before, /device:TPU:97 now
where the time goes in v4:
time: 23.6 us; the launch traced here: 23.2 us
  Pallas kernels  22.4 us (95%)
  local copies, waits for them, and re-layouts  0.8 us (3%)
    pallas_call x1, Pallas kernels, shards(): pl.pallas_call(functools.partial(kernel, segments, slabs), out_shape=tile...  22.4 us
    unnamed x1, local copies, waits for them, and re-layouts  0.8 us

profile of v4, /device:TPU:97, one launch (start us, length us, event | category | flops | bytes accessed | tf_op | source)
XLA Modules:
  0.0 23.2 jit_solution(16956432898058209131)
XLA Ops:
  0.0 22.4 %shard_map.46 = f32[4,256,128]{2,1,0:T(8,128)S(1)} custom-call(f32[4,256,128]{2,1,0:T(8,128)} %bitcast.16, f32[4,256,128]{2,1,0:T(8,128)} %bitcast.17, s32[4,32]{1,0:T(4,128)} %levels.1, f32[4]{0:T(128)} %table.1), custom_call_target="tpu_custom_call" | custom-call | tf_op jit(solution)/shard_map/pallas_call | solution.py:427
  22.4 0.8 %copy.6 = f32[1,32,4096]{2,1,0:T(8,128)} copy(f32[1,32,4096]{2,1,0:T(8,128)S(1)} %bitcast.15) | data formatting | bytes 1048576

commit v5 on v4

--- a/solution.py
+++ b/solution.py
@@ -227,7 +227,7 @@
     below, above = lax.rem(sp + 1, slabs), lax.rem(sp + slabs - 1, slabs)
     next_dev, prev_dev, down_dev, up_dev = (after, sp), (before, sp), (tm, below), (tm, above)
     even = lax.rem(sp, 2) == 0
-    lower_first = even | (sp == slabs - 1)
+    lower_first = (even & (sp != slabs // 2)) | (sp == slabs - 1) | (sp == 1)
 
     def back_row(i):
         first, count = BACK[i]

time: 23.6 us -> 23.3 us (0.987); the launches traced: 23.2 us -> 23.2 us
  no operation moved by 1% of the time
where the time goes in v5:
time: 23.3 us; the launch traced here: 23.2 us
  Pallas kernels  22.4 us (96%)
  local copies, waits for them, and re-layouts  0.8 us (3%)
    pallas_call x1, Pallas kernels, shards(): pl.pallas_call(functools.partial(kernel, segments, slabs), out_shape=tile...  22.4 us
    unnamed x1, local copies, waits for them, and re-layouts  0.8 us

profile of v5, /device:TPU:97, one launch (start us, length us, event | category | flops | bytes accessed | tf_op | source)
XLA Modules:
  0.0 23.2 jit_solution(10679111714826004592)
XLA Ops:
  0.0 22.4 %shard_map.46 = f32[4,256,128]{2,1,0:T(8,128)S(1)} custom-call(f32[4,256,128]{2,1,0:T(8,128)} %bitcast.16, f32[4,256,128]{2,1,0:T(8,128)} %bitcast.17, s32[4,32]{1,0:T(4,128)} %levels.1, f32[4]{0:T(128)} %table.1), custom_call_target="tpu_custom_call" | custom-call | tf_op jit(solution)/shard_map/pallas_call | solution.py:427
  22.4 0.8 %copy.6 = f32[1,32,4096]{2,1,0:T(8,128)} copy(f32[1,32,4096]{2,1,0:T(8,128)S(1)} %bitcast.15) | data formatting | bytes 1048576
